TPU v7x, 32 devices: a whole 2x2x4 slice. The times are simulated.
32 devices in a mesh: rows: 2 (over core), canvas: 16 (over z, y, x).
Axes of the slice: x: 2, y: 2, z: 4, core: 2. Of those that a mesh axis runs over, the one named last changes fastest.
Arguments:
- patch_embeddings: float32 [16, 64, 32, 384], P('canvas', 'rows'), may hold values from -12 to 12
- loss_sensitivity: float32 [16, 64, 32, 384], P('canvas', 'rows'), may hold values from -6 to 6
- patch_tallness: int32 [16, 4], P('canvas'), may hold values from 2 to 24, as said below
- triple_linear_map: float32 [384, 1152], replicated, may hold values from -0.3125 to 0.3125
- mixing_linear_map: float32 [384, 384], replicated, may hold values from -0.625 to 0.625
- expanding_linear: float32 [384, 1536], replicated, may hold values from -0.3125 to 0.3125
- contracting_linear: float32 [1536, 384], replicated, may hold values from -0.15625 to 0.15625
- triple_momentum: float32 [384, 1152], replicated, may hold values from -320 to 320
- mixing_momentum: float32 [384, 384], replicated, may hold values from -448 to 448
- expanding_momentum: float32 [384, 1536], replicated, may hold values from -320 to 320
- contracting_momentum: float32 [1536, 384], replicated, may hold values from -640 to 640
- auxiliary_entry_table: float32 [40, 384], replicated, may hold values from -3 to 3
- auxiliary_first_moment: float32 [40, 384], replicated, may hold values from -32 to 32
- auxiliary_second_moment: float32 [40, 384], replicated, may hold values from 157.2864 to 622.592
- logit_scaling: float32 [8], replicated, may hold values from 2 to 6
- temper_first_moment: float32 [8], replicated, may hold values from -128 to 128
- temper_second_moment: float32 [8], replicated, may hold values from 1736.704 to 6881.28
Outputs:
- block_result: float32 [16, 64, 32, 384], P('canvas', 'rows')
- gradient_input_tokens: float32 [16, 64, 32, 384], P('canvas', 'rows')
- gradient_query_key_value: float32 [384, 1152], replicated
- gradient_output_weight: float32 [384, 384], replicated
- gradient_up_weight: float32 [384, 1536], replicated
- gradient_down_weight: float32 [1536, 384], replicated
- momentum_qkv: float32 [384, 1152], replicated
- momentum_proj: float32 [384, 384], replicated
- momentum_fc1: float32 [384, 1536], replicated
- momentum_fc2: float32 [1536, 384], replicated
- new_qkv: float32 [384, 1152], replicated
- new_proj: float32 [384, 384], replicated
- new_fc1: float32 [384, 1536], replicated
- new_fc2: float32 [1536, 384], replicated
- copy_qkv: bfloat16 [384, 1152], replicated
- copy_proj: bfloat16 [384, 384], replicated
- copy_fc1: bfloat16 [384, 1536], replicated
- copy_fc2: bfloat16 [1536, 384], replicated
- small_first_new: float32 [40, 384], replicated
- small_second_new: float32 [40, 384], replicated
- small_new: float32 [40, 384], replicated
- temper_first_moment_fresh: float32 [8], replicated
- temper_second_moment_fresh: float32 [8], replicated
- temper_revised: float32 [8], replicated
- stream_rms: float32 [4], replicated
Inputs may be any that keep to these rules, and one draw needn't show every extreme that they name: `patch_tallness`: each row lists the 4 images of one canvas from top to bottom, each 32 columns wide; the heights sum to 64, and the third image has exactly 24 rows and holds rows 31 and 32.
All inputs are finite; a program needn't handle non-finite values.
Results may differ from a plain program's by a relative error of at most 0.001.
Values sent between devices are 32-bit elements; how exact they have to be, the bound alone decides.
A program may use at most 192 MiB of HBM per device.

v0:
```python
import functools
import math

import jax
import jax.numpy as jnp
from jax import lax
from jax.experimental import pallas as pl
from jax.experimental.pallas import tpu as pltpu
from jax.sharding import PartitionSpec as P

BF = jnp.bfloat16
F32 = jnp.float32
MESH_ID = pl.DeviceIdType.MESH

EPS = 1e-06
ROOT_HALF = 1.0 / math.sqrt(2.0)
ROOT_TWOPI = 1.0 / math.sqrt(2.0 * math.pi)
STEP = 10
MUON_RATE = 0.2
MUON_KEEP = 0.95
DECAY = 0.01
ADAM_RATE = 0.2
BETA1 = 0.9
BETA2 = 0.95
ADAM_FLOOR = 1e-08

HEADS = 8
HD = 48
D = HEADS * HD
COLS = 32
HALO = 4 * COLS
TILE = 256

N1G, N1S, N3G, N3S, N2G, N2S, SA, SL, SM, QB, KB, VB, PB, C1B, BG, BS, C2B, F2B = range(18)
F1B, K1R, K2R = 18, 22, 31
SMALL = 40
TABLE = 48


def halves(v):
    hi = v.astype(BF)
    return hi, (v - hi.astype(F32)).astype(BF)


def side(v):
    h, l = halves(v)
    return jnp.concatenate([h, l, h], axis=1)


def dot_nn(a, b):
    return lax.dot_general(a, b, (((1,), (0,)), ((), ())), preferred_element_type=F32)


def dot_nt(a, b):
    return lax.dot_general(a, b, (((1,), (1,)), ((), ())), preferred_element_type=F32)


def normalize(v):
    mean = jnp.mean(v, axis=1, keepdims=True)
    c = v - mean
    r = lax.rsqrt(jnp.mean(c * c, axis=1, keepdims=True) + EPS)
    return c * r, r


def normalize_back(e, xhat, r):
    return r * (
        e - jnp.mean(e, axis=1, keepdims=True) - xhat * jnp.mean(e * xhat, axis=1, keepdims=True)
    )


def gelu_parts(v):
    phi = 0.5 * (1.0 + lax.erf(v * ROOT_HALF))
    return v * phi, phi + v * jnp.exp(-0.5 * v * v) * ROOT_TWOPI


def eights(v):
    total = v[0:8]
    for i in range(8, v.shape[0], 8):
        total = total + v[i : i + 8]
    return total


def sweep(count, size, body):
    def one(i, carry):
        body(pl.multiple_of(i * size, size))
        return carry

    lax.fori_loop(0, count // size, one, 0)


def image_ends(tall_ref):
    e0 = tall_ref[0, 0]
    e1 = e0 + tall_ref[0, 1]
    return e0, e1, e1 + tall_ref[0, 2]


def slots(tall_ref, core, first_row, rows_all):
    e0, e1, e2 = image_ends(tall_ref)
    low = (jnp.where(core == 0, 0, e2), jnp.where(core == 0, e0, 0), e1)
    high = (jnp.where(core == 0, e0, rows_all), jnp.where(core == 0, e1, 0), e2)
    return [((a - first_row) * COLS, (b - first_row) * COLS) for a, b in zip(low, high)]


def span_mask(start, rows, lo, hi):
    token = start + lax.broadcasted_iota(jnp.int32, (rows, D), 0)
    return (token >= lo) & (token < hi)


def slot_masks(start, rows, spans):
    return [jnp.where(span_mask(start, rows, lo, hi), 1.0, 0.0).astype(BF) for lo, hi in spans]


def by_slot(v, masks):
    h, l = halves(v)
    parts = []
    for mask in masks:
        hm = h * mask
        parts += [hm, l * mask, hm]
    return parts


def whole_and_far(parts):
    return jnp.concatenate(parts, axis=1), jnp.concatenate([p[:, 128:] for p in parts], axis=1)


def mix_nt(parts, ref):
    every, far = whole_and_far(parts)
    corner = [ref[256:D, n * D + 128 : n * D + D] for n in range(len(parts))]
    return jnp.concatenate(
        [dot_nt(every, ref[0:256]), dot_nt(far, jnp.concatenate(corner, axis=1))], axis=1
    )


def mix_nn(parts, ref):
    every, far = whole_and_far(parts)
    corner = [ref[n * D + 128 : n * D + D, 256:D] for n in range(len(parts))]
    return jnp.concatenate(
        [dot_nn(every, ref[:, 0:256]), dot_nn(far, jnp.concatenate(corner, axis=0))], axis=1
    )


def slots_below(v, masks):
    h, l = halves(v)
    high = jnp.concatenate([h * mask for mask in masks], axis=1)
    return jnp.concatenate([high, high, jnp.concatenate([l * mask for mask in masks], axis=1)], axis=0)


def lane_head():
    return lax.broadcasted_iota(jnp.int32, (HD, D), 1) // HD


def lane_slot():
    return lax.broadcasted_iota(jnp.int32, (HD, D), 1) % HD


def fold(full):
    head = lane_head()
    total = jnp.where(head == 0, full[0:HD], 0.0)
    for h in range(1, HEADS):
        total = total + jnp.where(head == h, full[h * HD : h * HD + HD], 0.0)
    return total


def unfold(small):
    head = lane_head()
    return jnp.concatenate([jnp.where(head == h, small, 0.0) for h in range(HEADS)], axis=0)


def group_ones():
    a = lax.broadcasted_iota(jnp.int32, (D, D), 0) // HD
    b = lax.broadcasted_iota(jnp.int32, (D, D), 1) // HD
    return jnp.where(a == b, 1.0, 0.0).astype(BF)


def group_sum(v, ones):
    h = v.astype(BF)
    rest = v - h.astype(F32)
    m = rest.astype(BF)
    l = (rest - m.astype(F32)).astype(BF)
    return dot_nn(h, ones) + (dot_nn(m, ones) + dot_nn(l, ones))


def row_to_fold(row, ones):
    slot = lax.broadcasted_iota(jnp.int32, (HD, D), 0)
    return group_sum(jnp.where(lane_slot() == slot, jnp.broadcast_to(row, (HD, D)), 0.0), ones)


def fold_to_row(small):
    slot = lax.broadcasted_iota(jnp.int32, (HD, D), 0)
    return jnp.sum(jnp.where(lane_slot() == slot, small, 0.0), axis=0, keepdims=True)


def head_row(temp_ref):
    head = lax.broadcasted_iota(jnp.int32, (1, D), 1) // HD
    row = jnp.where(head == 0, temp_ref[0], 0.0)
    for h in range(1, HEADS):
        row = row + jnp.where(head == h, temp_ref[h], 0.0)
    return row


def project_kernel(tall_ref, x_ref, w_ref, tab_ref, q_ref, k_ref, v_ref, sums_ref, wcat, cross):
    step = pl.program_id(0)
    core = lax.axis_index("rows")
    rows_all = 2 * pl.num_programs(0) * TILE // COLS
    spans = slots(tall_ref, core, core * (rows_all // 2), rows_all)
    start = step * TILE

    @pl.when(step == 0)
    def _():
        def part(o):
            h, l = halves(w_ref[pl.ds(o, 64)])
            wcat[pl.ds(o, 64)] = h
            wcat[pl.ds(D + o, 64)] = h
            wcat[pl.ds(2 * D + o, 64)] = l

        sweep(D, 64, part)
        cross[...] = jnp.zeros_like(cross)
        sums_ref[...] = jnp.zeros_like(sums_ref)

    xhat, _ = normalize(x_ref[...])
    lhs = side(xhat * tab_ref[N1G : N1G + 1] + tab_ref[N1S : N1S + 1])
    qkv = dot_nn(lhs, wcat[...])
    q = qkv[:, 0:D] + tab_ref[QB : QB + 1]
    q_ref[...] = q
    k = qkv[:, D : 2 * D] + tab_ref[KB : KB + 1]
    k_ref[...] = k
    v_ref[...] = qkv[:, 2 * D : 3 * D] + tab_ref[VB : VB + 1]
    cross[...] += dot_nn(side(q.T), slots_below(k, slot_masks(start, TILE, spans)))
    for s, (lo, hi) in enumerate(spans):
        mask = span_mask(start, TILE, lo, hi)
        for n, v in enumerate((q, k)):
            row = HD + n
            sums_ref[s, row : row + 1] += jnp.sum(jnp.where(mask, v * v, 0.0), axis=0, keepdims=True)

    @pl.when(step == pl.num_programs(0) - 1)
    def _():
        for s in range(3):
            sums_ref[s, 0:HD] = fold(cross[:, s * D : s * D + D])


def project(tall, x, w, tab):
    tokens = x.shape[0]
    row = pl.BlockSpec((TILE, D), lambda i: (i, 0))
    return pl.pallas_call(
        project_kernel,
        grid=(tokens // TILE,),
        out_shape=[jax.ShapeDtypeStruct((tokens, D), F32)] * 3
        + [jax.ShapeDtypeStruct((3, HD + 8, D), F32)],
        in_specs=[
            pl.BlockSpec(memory_space=pltpu.SMEM),
            row,
            pl.BlockSpec((D, 3 * D), lambda i: (0, 0)),
            pl.BlockSpec((SMALL, D), lambda i: (0, 0)),
        ],
        out_specs=[row, row, row, pl.BlockSpec((3, HD + 8, D), lambda i: (0, 0, 0))],
        scratch_shapes=[pltpu.VMEM((3 * D, 3 * D), BF), pltpu.VMEM((D, 3 * D), F32)],
        compiler_params=pltpu.CompilerParams(vmem_limit_bytes=60 << 20),
    )(tall, x, w, tab)


ORDERS = ((0, 1, 2, 3), (1, 2, 0, 3), (2, 0, 1, 3))
EARLY, LATE = range(0, 3), range(3, 6)
PIECE = 256
GROUP = 1536
SHARD = D // 16
DMA = pltpu.SemaphoreType.DMA


class Links:
    def __init__(self):
        self.core = lax.axis_index("rows")
        chip = lax.axis_index("canvas")
        self.bits = (lax.axis_size("canvas") - 1).bit_length()
        self.mine = [lax.rem(lax.div(chip, 1 << b), 2) for b in range(self.bits)]
        self.there = [{"canvas": chip + (1 - 2 * m) * (1 << b)} for b, m in enumerate(self.mine)]
        self.twin = {"rows": 1 - self.core}

    def call(self):
        barrier = pltpu.get_barrier_semaphore()
        for other in [self.twin] + self.there:
            pl.semaphore_signal(barrier, inc=1, device_id=other, device_id_type=MESH_ID)

    def answer(self):
        pl.semaphore_wait(pltpu.get_barrier_semaphore(), self.bits + 1)

    def greet(self):
        self.call()
        self.answer()


def remote(src, dst, send, recv, other):
    return pltpu.make_async_remote_copy(
        src_ref=src,
        dst_ref=dst,
        send_sem=send,
        recv_sem=recv,
        device_id=other,
        device_id_type=MESH_ID,
    )


class Pieces:
    count = 6

    def __init__(self, links, lanes):
        self.links = links
        self.width = lanes // self.count

    def lanes(self, p):
        return slice(p * self.width, p * self.width + self.width)

    def bit(self, p, s):
        return ORDERS[p % 3][s]

    def start(self, p, s):
        at = 0
        for t in range(s):
            at = at + self.links.mine[self.bit(p, t)] * (D >> (t + 1))
        return at

    def held(self, p, s):
        return pl.ds(pl.multiple_of(self.start(p, s), 8), D >> s)


class Reduce(Pieces):
    def __init__(self, links, src, buf, work):
        super().__init__(links, src.shape[-1])
        self.src, self.buf = src, buf
        self.first, self.land, self.pair_sem, self.send_sem, self.recv_sem = work

    @classmethod
    def scratch(cls, lanes, bits):
        steps = max(bits, 4)
        return [
            pltpu.VMEM((D, lanes), F32),
            pltpu.VMEM((D - SHARD + (steps - 4) * SHARD, lanes), F32),
            DMA((2, cls.count)),
            DMA((cls.count, steps)),
            DMA((cls.count, steps)),
        ]

    def add(self, p, rows, src, src_rows):
        lanes = self.lanes(p)
        self.buf[rows, lanes] += src[src_rows, lanes]

    def pair(self, p):
        lanes = self.lanes(p)
        return remote(
            self.src.at[1 - self.links.core, :, lanes],
            self.first.at[:, lanes],
            self.pair_sem.at[0, p],
            self.pair_sem.at[1, p],
            self.links.twin,
        )

    def move(self, p, s):
        b = self.bit(p, s)
        half = D >> (s + 1)
        away = pl.multiple_of(self.start(p, s) + (1 - self.links.mine[b]) * half, 8)
        lanes = self.lanes(p)
        return remote(
            self.buf.at[pl.ds(away, half), lanes],
            self.land.at[pl.ds(D - (D >> s), half), lanes],
            self.send_sem.at[p, s],
            self.recv_sem.at[p, s],
            self.links.there[b],
        )

    def begin(self):
        for p in range(self.count):
            self.pair(p).start()

    def join(self, some):
        for p in some:
            self.pair(p).wait()
            self.add(p, pl.ds(0, D), self.first, pl.ds(0, D))
            self.move(p, 0).start()

    def launch(self):
        for p in range(self.count):
            self.move(p, 0).start()

    def down(self, s, some, last=3):
        for p in some:
            self.move(p, s).wait()
            self.add(p, self.held(p, s + 1), self.land, pl.ds(D - (D >> s), D >> (s + 1)))
            if s < last:
                self.move(p, s + 1).start()
        if s == 3:
            for b in range(4, self.links.bits):
                self.swap(b, some)

    def swap(self, b, some):
        at = pl.ds(D - SHARD + (b - 4) * SHARD, SHARD)
        copies = {}
        for p in some:
            lanes = self.lanes(p)
            copies[p] = remote(
                self.buf.at[self.held(p, 4), lanes],
                self.land.at[at, lanes],
                self.send_sem.at[p, b],
                self.recv_sem.at[p, b],
                self.links.there[b],
            )
            copies[p].start()
        for p in some:
            copies[p].wait()
            self.add(p, self.held(p, 4), self.land, at)


class Gather(Pieces):
    def __init__(self, links, whole, dst, work):
        super().__init__(links, whole.shape[1])
        self.whole, self.dst = whole, dst
        self.send_sem, self.recv_sem, self.out_sem = work

    @classmethod
    def scratch(cls, lanes):
        return [DMA((cls.count, 4)), DMA((cls.count, 4)), DMA((2, 3, cls.count))]

    def back(self, p, s):
        view = self.whole.at[self.held(p, s + 1), self.lanes(p)]
        return remote(
            view,
            view,
            self.send_sem.at[p, s],
            self.recv_sem.at[p, s],
            self.links.there[self.bit(p, s)],
        )

    def outs(self, p, n):
        mine = self.links.mine[self.bit(p, 0)]
        half = D // 2
        at = pl.multiple_of(half * (mine if n == 0 else 1 - mine), 8)
        rows = pl.ds(at, half)
        src = self.whole.at[rows, self.lanes(p)]
        dst = self.dst.at[self.links.core, rows, self.lanes(p)]
        sem = self.out_sem.at[n]
        return (
            pltpu.make_async_copy(src, dst, sem.at[0, p]),
            remote(src, dst, sem.at[1, p], sem.at[2, p], self.links.twin),
        )

    def begin(self, some):
        for p in some:
            self.back(p, 3).start()

    def up(self, s, some):
        for p in some:
            self.back(p, s).wait()
            if s > 0:
                self.back(p, s - 1).start()
            if s < 2:
                for copy in self.outs(p, 1 - s):
                    copy.start()

    def end(self):
        for n in range(2):
            for p in range(self.count):
                for copy in self.outs(p, n):
                    copy.wait()


class Turn(Pieces):
    def __init__(self, links, rest, whole, work):
        super().__init__(links, whole.shape[1])
        self.rest, self.whole = rest, whole
        self.land, self.send_sem, self.recv_sem = work

    @classmethod
    def scratch(cls, lanes, bits):
        steps = max(bits, 4) - 3
        return [
            pltpu.VMEM((steps * SHARD, lanes), F32),
            DMA((cls.count, steps)),
            DMA((cls.count, steps)),
        ]

    def move(self, p, n):
        lanes = self.lanes(p)
        if n == 0:
            b = self.bit(p, 3)
            at = pl.multiple_of((1 - self.links.mine[b]) * SHARD, 8)
            src = self.rest.at[pl.ds(at, SHARD), lanes]
        else:
            b = 3 + n
            src = self.whole.at[self.held(p, 4), lanes]
        return remote(
            src,
            self.land.at[n * SHARD : n * SHARD + SHARD, lanes],
            self.send_sem.at[p, n],
            self.recv_sem.at[p, n],
            self.links.there[b],
        )

    def begin(self):
        for p in range(self.count):
            self.move(p, 0).start()

    def end(self, some):
        for p in some:
            lanes = self.lanes(p)
            at = pl.multiple_of(self.links.mine[self.bit(p, 3)] * SHARD, 8)
            self.move(p, 0).wait()
            self.whole[self.held(p, 4), lanes] = (
                self.rest[pl.ds(at, SHARD), lanes] + self.land[0:SHARD, lanes]
            )
        for n in range(1, self.links.bits - 3):
            for p in some:
                self.move(p, n).start()
            for p in some:
                lanes = self.lanes(p)
                self.move(p, n).wait()
                self.whole[self.held(p, 4), lanes] += self.land[n * SHARD : n * SHARD + SHARD, lanes]


def row_flags(tall_ref, rows_all):
    ends = image_ends(tall_ref)

    def above(row):
        first = (row == 0) | (row == ends[0]) | (row == ends[1]) | (row == ends[2])
        return jnp.where(first, 0.0, 1.0)

    def below(row):
        return jnp.where(row + 1 == rows_all, 0.0, above(row + 1))

    return above, below


def middle_kernel(
    tall_ref,
    temp_ref,
    x_hbm,
    dy_hbm,
    v_hbm,
    sums_ref,
    wp_ref,
    w1_hbm,
    w2_ref,
    tab_ref,
    out_hbm,
    ds1_hbm,
    dmx_hbm,
    dwp_ref,
    shard_ref,
    gtab_ref,
    probs_ref,
    unit_ref,
    gprob_ref,
    joint_ref,
    wpv,
    wph,
    w1c,
    w2c,
    pcat,
    mixed,
    s1,
    li,
    act,
    slope,
    mid,
    s2,
    ds2,
    gp,
    n2c,
    dzc,
    b1_ref,
    b1g_ref,
    acc,
    cross,
    x_ref,
    dy_ref,
    v_ref,
    flags,
    nt,
    dt,
    peer_ref,
    dw_ref,
    load_sem,
    store_sem,
    edge_sem,
    *work,
):
    links = Links()
    core = links.core
    wide = x_ref.shape[0]
    tokens = wide - HALO
    dw1_ref, dw2_ref = dw_ref.at[0], dw_ref.at[1]
    reduce = Reduce(links, dw_ref, dw_ref.at[core], work)
    w1_ref = work[0]
    lo_ = x_ref
    own = pl.ds(pl.multiple_of(core * HALO, HALO), tokens)
    pairs = ((w1_hbm, w1_ref), (v_hbm, v_ref.at[own]), (x_hbm, x_ref.at[own]), (dy_hbm, dy_ref.at[own]))
    loads = [pltpu.make_async_copy(a, b, load_sem.at[i]) for i, (a, b) in enumerate(pairs)]
    for load in loads:
        load.start()
    links.call()
    edge = pl.ds(pl.multiple_of((1 - core) * (tokens - HALO), HALO), HALO)
    far = pl.ds(pl.multiple_of(core * tokens, HALO), HALO)
    pairs = (
        (sums_ref.at[2], peer_ref),
        (v_hbm.at[edge], v_ref.at[far]),
        (x_hbm.at[edge], x_ref.at[far]),
        (dy_hbm.at[edge], dy_ref.at[far]),
    )
    edges = [
        remote(a, b, edge_sem.at[0, i], edge_sem.at[1, i], links.twin)
        for i, (a, b) in enumerate(pairs)
    ]
    own_rows = tokens // COLS
    rows_wide = wide // COLS
    rows_all = 2 * own_rows
    first_row = core * (own_rows - HALO // COLS)
    own_off = pl.multiple_of(core * HALO, HALO)
    mlp = w1_hbm.shape[1]
    spans = slots(tall_ref, core, first_row, rows_all)
    above, below = row_flags(tall_ref, rows_all)

    def tab(r):
        return tab_ref[r : r + 1]

    def is_own(row):
        return (row >= core * (HALO // COLS)) & (row < core * (HALO // COLS) + own_rows)

    loads[0].wait()

    def part_1(o):
        rows = pl.ds(o, 64)
        h, l = halves(w1_ref[rows])
        w1c[rows] = h
        w1c[pl.ds(D + o, 64)] = h
        w1c[pl.ds(2 * D + o, 64)] = l

    sweep(D, 64, part_1)
    links.answer()
    for copy in edges:
        copy.start()

    def part_p(o):
        rows = pl.ds(o, 192)
        h, l = halves(wp_ref[rows])
        wpv[rows] = h
        wpv[pl.ds(D + o, 192)] = h
        wpv[pl.ds(2 * D + o, 192)] = l
        wph[rows, 0:D] = h
        wph[rows, D : 2 * D] = h
        wph[rows, 2 * D : 3 * D] = l

    sweep(D, 192, part_p)

    def part_2(o):
        rows = pl.ds(o, 256)
        h, l = halves(w2_ref[rows])
        w2c[rows, 0:D] = h
        w2c[rows, D : 2 * D] = h
        w2c[rows, 2 * D : 3 * D] = l

    sweep(mlp, 256, part_2)

    edges[0].wait()
    ones = group_ones()
    temp = head_row(temp_ref)
    joint_ref[...] = sums_ref[2] + peer_ref[...]

    def probabilities(s, carry):
        sums = jnp.where(s == 2, joint_ref[...], sums_ref[s])
        inv_q = lax.rsqrt(sums[HD : HD + 1] + EPS)
        inv_k = lax.rsqrt(sums[HD + 1 : HD + 2] + EPS)
        unit = sums[0:HD] * row_to_fold(inv_q, ones) * inv_k
        unit_ref[s] = unit
        weight = jnp.exp(temp * unit)
        probs = weight / group_sum(weight, ones)
        probs_ref[s] = probs
        h, l = halves(unfold(probs))
        lanes = pl.ds(pl.multiple_of(3 * D * s, 128), 3 * D)
        pcat[:, lanes] = jnp.concatenate([h, h, l], axis=1)
        return carry

    lax.fori_loop(0, 3, probabilities, 0)

    acc[...] = jnp.zeros_like(acc)
    gtab_ref[...] = jnp.zeros_like(gtab_ref)

    def add(r, v):
        acc[8 * r : 8 * r + 8] += v

    for copy in loads[1:] + edges[1:]:
        copy.wait()

    def own_part(o, size):
        token = o + lax.broadcasted_iota(jnp.int32, (size, D), 0)
        return jnp.where((token >= own_off) & (token < own_off + tokens), 1.0, 0.0)

    def attend(o):
        size = wide // 3
        mix = mix_nt(by_slot(v_ref[pl.ds(o, size)], slot_masks(o, size, spans)), pcat)
        mixed[pl.ds(o, size)] = mix
        z = dot_nn(side(mix), wpv[...]) + tab(PB)
        rows = pl.ds(o, size)
        branch = tab(SA) * z
        stream = x_ref[rows] + branch
        s1[rows] = stream
        xhat, _ = normalize(stream)
        li[pl.ds(pl.multiple_of(o + COLS, COLS), size)] = xhat * tab(N3G) + tab(N3S)
        add(41, eights(own_part(o, size) * branch * branch))

    sweep(wide, wide // 3, attend)

    pad = jnp.zeros((COLS, D), F32)
    for buf in (li, mid, gp, ds2):
        buf[0:COLS] = pad
        buf[wide + COLS : wide + 2 * COLS] = pad

    for r in range(rows_wide):
        row = first_row + r
        mine = jnp.where(is_own(r), 1.0, 0.0)
        for n, flag in enumerate((above(row), below(row), mine)):
            flags[n, r * COLS : r * COLS + COLS] = jnp.full((COLS, 128), flag, F32)

    block = 12 * COLS
    col = lax.rem(lax.broadcasted_iota(jnp.int32, (block + 2 * COLS, 128), 0), COLS)

    def convolve(src, base, flip, scale, visit, other=None, events=()):
        def one(n, carry):
            for when, event in events:
                pl.when(n == when)(event)
            lanes = pl.ds(pl.multiple_of(lax.rem(n, 3) * 128, 128), 128)
            m = lax.div(n, 3)
            place = lax.div((m - 1) * (m - 2), 2) + 2 * core * m * (2 - m) + (1 - core) * m * (m - 1)
            o = pl.multiple_of(place * block, block)
            rows = pl.ds(o, block)
            taps = [tab_ref[base + t : base + t + 1, lanes] for t in range(9)]
            if flip:
                taps = taps[::-1]
            if scale is not None:
                taps = [t * tab_ref[scale : scale + 1, lanes] for t in taps]
            u = src[pl.ds(o, block + 2 * COLS), lanes]
            left = jnp.where(col == 0, 0.0, pltpu.roll(u, 1, 0))
            right = jnp.where(col == COLS - 1, 0.0, pltpu.roll(u, block + 2 * COLS - 1, 0))
            up, down = flags[0, rows], flags[1, rows]

            def line(a):
                cut = slice(a * COLS, a * COLS + block)
                return left[cut] * taps[3 * a] + u[cut] * taps[3 * a + 1] + right[cut] * taps[3 * a + 2]

            visit(o, rows, lanes, line(1) + up * line(0) + down * line(2))
            if other is not None:
                near = other[pl.ds(o, block + 2 * COLS), lanes]
                mine = flags[2, rows]
                held = (
                    mine * up * near[0:block],
                    mine * near[COLS : COLS + block],
                    mine * down * near[2 * COLS : 2 * COLS + block],
                )
                inner = slice(COLS, COLS + block)
                for a in range(3):
                    for b, view in enumerate((right, u, left)):
                        t = 8 * (base + 3 * a + b)
                        acc[t : t + 8, lanes] += eights(view[inner] * held[a])
            return carry

        lax.fori_loop(0, 3 * (wide // block), one, 0)

    def first(o, rows, lanes, value):
        at = pl.ds(o + COLS, block)
        a, s = gelu_parts(value + tab_ref[C1B : C1B + 1, lanes])
        act[rows, lanes] = a
        slope[rows, lanes] = s
        mid[at, lanes] = a * tab_ref[BG : BG + 1, lanes] + tab_ref[BS : BS + 1, lanes]

    convolve(li, K1R, False, None, first)

    def second(o, rows, lanes, value):
        value = value + tab_ref[C2B : C2B + 1, lanes]
        lo_[rows, lanes] = value
        branch = tab_ref[SL : SL + 1, lanes] * value
        s2[rows, lanes] = s1[rows, lanes] + branch
        acc[8 * 42 : 8 * 42 + 8, lanes] += eights(flags[2, rows] * branch * branch)

    convolve(mid, K2R, False, None, second)

    dw1_ref[...] = jnp.zeros_like(dw1_ref)
    dw2_ref[...] = jnp.zeros_like(dw2_ref)
    b1g_ref[...] = jnp.zeros_like(b1g_ref)
    for i in range(mlp // D):
        b1_ref[0:1, i * D : i * D + D] = tab(F1B + i)

    def feed(o):
        here = pl.ds(o, TILE)
        xhat, _ = normalize(s2[here])
        n2 = xhat * tab(N2G) + tab(N2S)
        n2c[...] = side(n2)
        dz = tab(SM) * dy_ref[here]
        dzc[...] = side(dz)
        nt[...] = side(n2.T)
        dt[...] = side(dz.T)
        add(F2B, eights(dz))

        padded = pl.ds(pl.multiple_of(o + COLS, COLS), TILE)
        gp[COLS : COLS + TILE] = jnp.broadcast_to(tab(F2B), (TILE, D))
        ds2[padded] = jnp.zeros((TILE, D), F32)

        def chunk(j):
            return pl.ds(pl.multiple_of(j, PIECE), PIECE)

        def enter(j):
            return dot_nn(n2c[...], w1c[:, chunk(j)]), dot_nt(dzc[...], w2c[chunk(j)])

        def chunks(first):
            raw = dn = 0.0
            ready = enter(first)
            for j in range(0, GROUP, PIECE):
                lanes = chunk(first + j)
                pre, dh = ready
                if j + PIECE < GROUP:
                    ready = enter(first + j + PIECE)
                a, slope_j = gelu_parts(pre + b1_ref[0:1, lanes])
                dp = dh * slope_j
                ah, al = halves(a)
                ph, pl_ = halves(dp)
                w2h, w2l = w2c[lanes, 0:D], w2c[lanes, 2 * D : 3 * D]
                raw = raw + (dot_nn(ah, w2h) + (dot_nn(al, w2h) + dot_nn(ah, w2l)))
                w1h, w1l = w1c[0:D, lanes], w1c[2 * D : 3 * D, lanes]
                dn = dn + (dot_nt(ph, w1h) + (dot_nt(pl_, w1h) + dot_nt(ph, w1l)))
                b1g_ref[:, lanes] += eights(dp)
                dw1_ref[:, lanes] += dot_nn(nt[...], jnp.concatenate([ph, ph, pl_], axis=0))
                dw2_ref[:, lanes] += dot_nn(dt[...], jnp.concatenate([ah, ah, al], axis=0))
            gp[COLS : COLS + TILE] += raw
            ds2[padded] += dn

        sweep(mlp, GROUP, chunks)
        raw, dn = gp[COLS : COLS + TILE], ds2[padded]
        dy = dy_ref[here]
        xhat, r = normalize(s2[here])
        ds2[pl.ds(pl.multiple_of(o + COLS, COLS), TILE)] = dy + normalize_back(dn * tab(N2G), xhat, r)
        branch = tab(SM) * raw
        result = s2[here] + branch
        s2[here] = result
        add(40, eights(result * result))
        add(43, eights(branch * branch))
        add(SM, eights(dy * raw))
        add(N2G, eights(dn * xhat))
        add(N2S, eights(dn))

    def feed_one(i, carry):
        feed(pl.multiple_of(own_off + i * TILE, 128))
        return carry

    lax.fori_loop(0, tokens // TILE, feed_one, 0)
    reduce.begin()
    stores = [pltpu.make_async_copy(s2.at[own], out_hbm, store_sem.at[0])]
    stores[0].start()
    edge = HALO // 2
    rest = pl.multiple_of(COLS + (1 - core) * (tokens + edge), COLS)
    ds2[pl.ds(rest, edge)] = jnp.zeros((edge, D), F32)
    rows_out = pl.multiple_of(COLS + own_off + (1 - core) * (tokens - edge), COLS)
    rows_in = pl.multiple_of(COLS + edge + core * (tokens - edge), COLS)
    turned = remote(
        ds2.at[pl.ds(rows_out, edge)],
        ds2.at[pl.ds(rows_in, edge)],
        edge_sem.at[0, 4],
        edge_sem.at[1, 4],
        links.twin,
    )
    turned.start()

    def third(o, rows, lanes, value):
        grad = value * tab_ref[BG : BG + 1, lanes] * slope[rows, lanes]
        gp[pl.ds(o + COLS, block), lanes] = grad
        held = flags[2, rows] * value
        acc[8 * BG : 8 * BG + 8, lanes] += eights(held * act[rows, lanes])
        acc[8 * BS : 8 * BS + 8, lanes] += eights(held)
        acc[8 * C1B : 8 * C1B + 8, lanes] += eights(flags[2, rows] * grad)

    convolve(
        ds2,
        K2R,
        True,
        SL,
        third,
        mid,
        ((5, lambda: reduce.join(EARLY)), (6, turned.wait), (8, lambda: reduce.join(LATE))),
    )

    def fourth(o, rows, lanes, value):
        slope[rows, lanes] = value

    convolve(gp, K1R, True, None, fourth, li, ((6, lambda: reduce.down(0, EARLY, 2)),))

    dwp_ref[...] = jnp.zeros_like(dwp_ref)
    cross[...] = jnp.zeros_like(cross)

    def back(step):
        o = pl.multiple_of(own_off + step * TILE, 128)

        here_wide = pl.ds(o, TILE)
        xhat, r = normalize(s1[here_wide])
        grad = slope[here_wide]
        grad_two = ds2[pl.ds(pl.multiple_of(o + COLS, COLS), TILE)]
        result = grad_two + normalize_back(grad * tab(N3G), xhat, r)
        slope[here_wide] = result
        add(N3G, eights(grad * xhat))
        add(N3S, eights(grad))
        add(SL, eights(grad_two * lo_[here_wide]))
        add(C2B, eights(grad_two))
        add(PB, eights(result))
        dmx = dot_nt(side(tab(SA) * result), wph[...])
        act[here_wide] = dmx
        h, l = halves(result)
        dwp_ref[...] += dot_nn(side(mixed[pl.ds(o, TILE)].T), jnp.concatenate([h, h, l], axis=0))
        cross[...] += dot_nn(side(dmx.T), slots_below(v_ref[pl.ds(o, TILE)], slot_masks(o, TILE, spans)))

    def back_two(step, carry):
        back(2 * step)
        back(2 * step + 1)
        pl.when(step == 0)(lambda: reduce.down(0, LATE, 2))
        pl.when(step == 0)(lambda: reduce.down(1, EARLY, 2))
        return carry

    lax.fori_loop(0, tokens // TILE // 2, back_two, 0)
    reduce.down(1, LATE, 2)
    for src, dst in ((slope, ds1_hbm), (act, dmx_hbm)):
        stores.append(pltpu.make_async_copy(src.at[own], dst, store_sem.at[len(stores)]))
        stores[-1].start()
    for s in range(3):
        gprob_ref[s] = fold(cross[:, s * D : s * D + D])

    def total(r):
        return jnp.sum(acc[8 * r : 8 * r + 8], axis=0, keepdims=True)

    for r in (N3G, N3S, N2G, N2S, SL, SM, C1B, BG, BS, F2B, 40, 41, 42, 43):
        gtab_ref[r : r + 1] = total(r)
    for t in range(9):
        gtab_ref[K1R + t : K1R + t + 1] = total(K1R + t)
        gtab_ref[K2R + t : K2R + t + 1] = total(K2R + t) * tab(SL)
    gtab_ref[C2B : C2B + 1] = total(C2B) * tab(SL)
    gtab_ref[PB : PB + 1] = total(PB) * tab(SA)
    raw = dwp_ref[...]
    gtab_ref[SA : SA + 1] = jnp.sum(raw * wp_ref[...], axis=0, keepdims=True) + total(PB) * tab(PB)
    dwp_ref[...] = raw * tab(SA)
    for i in range(mlp // D):
        gtab_ref[F1B + i : F1B + i + 1] = jnp.sum(b1g_ref[:, i * D : i * D + D], axis=0, keepdims=True)
    reduce.down(2, EARLY, 2)
    reduce.down(2, LATE, 2)
    for p in range(reduce.count):
        lanes = reduce.lanes(p)
        shard_ref[:, lanes] = reduce.buf[reduce.held(p, 3), lanes]
    for copy in stores:
        copy.wait()


def middle(tall, temp, x, dy, v, sums, wp, w1, w2, tab):
    tokens = x.shape[0]
    wide = tokens + HALO
    mlp = w1.shape[1]
    smem = pl.BlockSpec(memory_space=pltpu.SMEM)
    vmem = pl.BlockSpec(memory_space=pltpu.VMEM)
    anywhere = pl.BlockSpec(memory_space=pl.ANY)

    def f(*shape):
        return jax.ShapeDtypeStruct(shape, F32)

    def s(*shape):
        return pltpu.VMEM(shape, F32)

    def b(*shape):
        return pltpu.VMEM(shape, BF)

    padded = s(wide + 2 * COLS, D)
    return pl.pallas_call(
        middle_kernel,
        out_shape=[
            f(tokens, D),
            f(tokens, D),
            f(tokens, D),
            f(D, D),
            f(2 * SHARD, mlp),
            f(TABLE, D),
            f(3, HD, D),
            f(3, HD, D),
            f(3, HD, D),
            f(*sums.shape[1:]),
        ],
        in_specs=[smem, smem] + [anywhere] * 3 + [vmem, vmem, anywhere, vmem, vmem],
        out_specs=[anywhere] * 3 + [vmem] * 7,
        scratch_shapes=[
            b(3 * D, D),
            b(D, 3 * D),
            b(3 * D, mlp),
            b(mlp, 3 * D),
            b(D, 9 * D),
            s(wide, D),
            s(wide, D),
            padded,
            s(wide, D),
            s(wide, D),
            padded,
            s(wide, D),
            padded,
            padded,
            b(TILE, 3 * D),
            b(TILE, 3 * D),
            s(8, mlp),
            s(8, mlp),
            s(8 * TABLE, D),
            s(D, 3 * D),
            s(wide, D),
            s(wide, D),
            s(wide, D),
            s(3, wide, 128),
            b(D, 3 * TILE),
            b(D, 3 * TILE),
            s(*sums.shape[1:]),
            s(2, D, mlp),
            DMA((4,)),
            DMA((3,)),
            DMA((2, 5)),
        ]
        + Reduce.scratch(mlp, (lax.axis_size("canvas") - 1).bit_length()),
        compiler_params=pltpu.CompilerParams(
            collective_id=0, has_side_effects=True, vmem_limit_bytes=60 << 20
        ),
    )(tall, temp, x, dy, v, sums, wp, w1, w2, tab)


def finish_kernel(
    tall_ref,
    temp_ref,
    x_ref,
    q_ref,
    k_ref,
    ds1_ref,
    dmx_ref,
    sums_ref,
    peer_ref,
    probs_ref,
    unit_ref,
    gprob_ref,
    w_ref,
    tab_ref,
    gtab_ref,
    dwp_ref,
    shard_ref,
    dx_ref,
    end_ref,
    town_ref,
    sum_hbm,
    wh,
    wl,
    pv,
    cv,
    ch,
    side_rows,
    acc,
    gpeer_ref,
    whole,
    dw_ref,
    otab_ref,
    end_first,
    tab_first,
    gsend,
    grecv,
    pair_sem,
    *work,
):
    step = pl.program_id(0)
    last = pl.num_programs(0) - 1
    links = Links()
    core = links.core
    turn = Turn(links, shard_ref, whole, work[:3])
    gather = Gather(links, whole, sum_hbm, work[3:])
    rows_all = 2 * pl.num_programs(0) * TILE // COLS
    spans = slots(tall_ref, core, core * (rows_all // 2), rows_all)
    start = step * TILE

    def tab(r):
        return tab_ref[r : r + 1]

    @pl.when(step == 0)
    def _():
        links.greet()
        swap = remote(gprob_ref.at[2], gpeer_ref, gsend, grecv, links.twin)
        swap.start()
        turn.begin()

        def part(o):
            h, l = halves(w_ref[pl.ds(o, 64)])
            wh[pl.ds(o, 64)] = h
            wl[pl.ds(o, 64)] = l

        sweep(D, 64, part)
        dw_ref[...] = jnp.zeros_like(dw_ref)
        dw_ref[1, :, D : 2 * D] = dwp_ref[...]
        acc[...] = jnp.zeros_like(acc)
        ones = group_ones()
        temp = head_row(temp_ref)
        swap.wait()

        def slot(s, heat):
            sums = jnp.where(s == 2, peer_ref[...], sums_ref[s])
            grad = gprob_ref[s] + jnp.where(s == 2, gpeer_ref[...], 0.0)
            inv_q = lax.rsqrt(sums[HD : HD + 1] + EPS)
            inv_k = lax.rsqrt(sums[HD + 1 : HD + 2] + EPS)
            probs = probs_ref[s]
            unit = unit_ref[s]
            scores = probs * (grad - group_sum(probs * grad, ones))
            part_heat = jnp.sum(scores * unit, axis=0, keepdims=True)
            heat = heat + jnp.where((s < 2) | (core == 0), part_heat, 0.0)
            pull = temp * scores
            both = pull * unit
            query = fold_to_row(group_sum(both, ones)) * inv_q * inv_q
            key = jnp.sum(both, axis=0, keepdims=True) * inv_k * inv_k
            side_rows[pl.ds(pl.multiple_of(8 * s, 8), 8)] = jnp.concatenate(
                [query, key, jnp.zeros((6, D), F32)], axis=0
            )
            across = pl.ds(pl.multiple_of(3 * D * s, 128), 3 * D)
            h, l = halves(unfold(pull * row_to_fold(inv_q, ones) * inv_k))
            cv[across] = jnp.concatenate([h, h, l], axis=0)
            ch[:, across] = jnp.concatenate([h, h, l], axis=1)
            h, l = halves(unfold(probs))
            pv[across] = jnp.concatenate([h, h, l], axis=0)
            return heat

        heat = lax.fori_loop(0, 3, slot, jnp.zeros((1, D), F32))
        otab_ref[...] = gtab_ref[...]
        otab_ref[44:45] = heat

    masks = [span_mask(start, TILE, lo, hi) for lo, hi in spans]
    factors = slot_masks(start, TILE, spans)

    def rows_of(r):
        return sum(jnp.where(mask, side_rows[8 * s + r : 8 * s + r + 1], 0.0) for s, mask in enumerate(masks))

    def at(n, *events):
        @pl.when(step == n)
        def _():
            for event, *args in events:
                event(*args)

    q, k = q_ref[...], k_ref[...]
    dq = mix_nt(by_slot(k, factors), ch) - q * rows_of(0)
    dk = mix_nn(by_slot(q, factors), cv) - k * rows_of(1)
    dv = mix_nn(by_slot(dmx_ref[...], factors), pv)
    dqkv = jnp.concatenate([dq, dk, dv], axis=1)
    at(0, (turn.end, EARLY), (gather.begin, EARLY))
    at(1, (gather.up, 3, EARLY))
    at(2, (gather.up, 2, LATE))
    at(3, (gather.up, 1, LATE))

    h, l = halves(dqkv)
    dn = dot_nt(h, wh[...]) + (dot_nt(l, wh[...]) + dot_nt(h, wl[...]))
    xhat, r = normalize(x_ref[...])
    nt = side((xhat * tab(N1G) + tab(N1S)).T)
    grads = dot_nn(nt, jnp.concatenate([h, h, l], axis=0))
    dw_ref[0] += grads[:, 0 : 2 * D]
    dw_ref[1, :, 0:D] += grads[:, 2 * D : 3 * D]
    dx_ref[...] = ds1_ref[...] + normalize_back(dn * tab(N1G), xhat, r)
    acc[0:8] += eights(dn * xhat)
    acc[8:16] += eights(dn)
    for i, v in enumerate((dq, dk, dv)):
        acc[16 + 8 * i : 24 + 8 * i] += eights(v)

    at(0, (turn.end, LATE), (gather.begin, LATE))
    at(1, (gather.up, 3, LATE), (gather.up, 2, EARLY))
    at(2, (gather.up, 1, EARLY))

    @pl.when(step == last)
    def _():
        for i, r in enumerate((N1G, N1S, QB, KB, VB)):
            otab_ref[r : r + 1] = jnp.sum(acc[8 * i : 8 * i + 8], axis=0, keepdims=True)
        trows = tab_first.shape[0]
        near = pl.ds(pl.multiple_of(core * trows, 8), trows)
        far = pl.ds(pl.multiple_of((1 - core) * trows, 8), trows)
        pairs = [(otab_ref.at[far], tab_first)]
        for p in range(end_first.shape[1] // 128):
            lanes = slice(p * 128, p * 128 + 128)
            pairs.append((dw_ref.at[1 - core, :, lanes], end_first.at[:, lanes]))
        copies = [
            remote(a, b, pair_sem.at[0, i], pair_sem.at[1, i], links.twin)
            for i, (a, b) in enumerate(pairs)
        ]
        for copy in copies:
            copy.start()
        gather.up(0, EARLY)
        gather.up(0, LATE)
        for copy in copies:
            copy.wait()
        town_ref[...] = otab_ref[near] + tab_first[...]
        end_ref[...] = dw_ref[core] + end_first[...]
        gather.end()


def finish(tall, temp, x, q, k, ds1, dmx, sums, peer, probs, unit, gprob, w, tab, gtab, dwp, shard):
    tokens = x.shape[0]
    smem = pl.BlockSpec(memory_space=pltpu.SMEM)
    anywhere = pl.BlockSpec(memory_space=pl.ANY)
    row = pl.BlockSpec((TILE, D), lambda i: (i, 0))
    bits = (lax.axis_size("canvas") - 1).bit_length()

    def whole(v):
        return pl.BlockSpec(v.shape, lambda i: (0,) * v.ndim)

    fixed = (sums, peer, probs, unit, gprob, w, tab, gtab, dwp, shard)
    return pl.pallas_call(
        finish_kernel,
        grid=(tokens // TILE,),
        out_shape=[
            jax.ShapeDtypeStruct((tokens, D), F32),
            jax.ShapeDtypeStruct((D, 2 * D), F32),
            jax.ShapeDtypeStruct((TABLE // 2, D), F32),
            jax.ShapeDtypeStruct((2, D, shard.shape[1]), F32),
        ],
        in_specs=[smem, smem] + [row] * 5 + [whole(v) for v in fixed],
        out_specs=[
            row,
            pl.BlockSpec((D, 2 * D), lambda i: (0, 0)),
            pl.BlockSpec((TABLE // 2, D), lambda i: (0, 0)),
            anywhere,
        ],
        scratch_shapes=[
            pltpu.VMEM((D, 3 * D), BF),
            pltpu.VMEM((D, 3 * D), BF),
            pltpu.VMEM((9 * D, D), BF),
            pltpu.VMEM((9 * D, D), BF),
            pltpu.VMEM((D, 9 * D), BF),
            pltpu.VMEM((24, D), F32),
            pltpu.VMEM((40, D), F32),
            pltpu.VMEM(gprob.shape[1:], F32),
            pltpu.VMEM((D, shard.shape[1]), F32),
            pltpu.VMEM((2, D, 2 * D), F32),
            pltpu.VMEM((TABLE, D), F32),
            pltpu.VMEM((D, 2 * D), F32),
            pltpu.VMEM((TABLE // 2, D), F32),
            DMA,
            DMA,
            DMA((2, 1 + 2 * D // 128)),
        ]
        + Turn.scratch(shard.shape[1], bits)
        + Gather.scratch(shard.shape[1]),
        compiler_params=pltpu.CompilerParams(
            collective_id=1, has_side_effects=True, vmem_limit_bytes=60 << 20
        ),
    )(tall, temp, x, q, k, ds1, dmx, *fixed)


NS_A, NS_B, NS_C = 3.4445, -4.7750, 2.0315


def times(a, b):
    return dot_nn(
        jnp.concatenate([a[0], a[1], a[0]], axis=1), jnp.concatenate([b[0], b[0], b[1]], axis=0)
    )


def mirrored(left, corner):
    edge = left.shape[1]
    return jnp.concatenate([left, jnp.concatenate([left[edge:].T, corner], axis=0)], axis=1)


EDGE = 2 * 128


def times_symmetric(a, b):
    lhs = jnp.concatenate([a[0], a[1], a[0]], axis=1)
    rhs = jnp.concatenate([b[0], b[0], b[1]], axis=0)
    return mirrored(dot_nn(lhs, rhs[:, :EDGE]), dot_nn(lhs[EDGE:], rhs[:, EDGE:]))


def gram_of(h, l):
    left = dot_nt(h, h[:EDGE]) + (dot_nt(l, h[:EDGE]) + dot_nt(h, l[:EDGE]))
    he, le = h[EDGE:], l[EDGE:]
    return mirrored(left, dot_nt(he, he) + (dot_nt(le, he) + dot_nt(he, le)))


def inverse_norm(v):
    total = jnp.sum(jnp.sum(v * v, axis=0, keepdims=True), axis=1, keepdims=True)
    return 1.0 / (jnp.sqrt(total) + 1e-07)


def wide_kernel(
    end_hbm,
    tab_hbm,
    mid_hbm,
    m1_hbm,
    m2_hbm,
    sum_hbm,
    otab_hbm,
    orth_hbm,
    xs,
    x,
    m1,
    m2,
    xc,
    poly,
    tbuf,
    tland,
    load_sem,
    tsend,
    trecv,
    tout,
    buf,
    own_sem,
    *work,
):
    links = Links()
    core = links.core
    reduce = Reduce(links, buf, buf, work[:5])
    gather = Gather(links, work[0], sum_hbm, work[5:])
    own = pltpu.make_async_copy(end_hbm, buf, own_sem)
    own.start()
    wide = m1.shape[1]
    blocks = wide // D
    trows = tbuf.shape[0]
    near = pl.ds(pl.multiple_of(core * trows, 8), trows)
    pairs = ((mid_hbm.at[core], x), (m1_hbm, m1), (m2_hbm, m2), (tab_hbm, tbuf))
    loads = [pltpu.make_async_copy(a, b, load_sem.at[i]) for i, (a, b) in enumerate(pairs)]
    for load in loads:
        load.start()
    links.greet()
    own.wait()
    reduce.launch()

    def table(n):
        return remote(tbuf, tland.at[n], tsend.at[n], trecv.at[n], links.there[n])

    def table_land(n):
        table(n).wait()
        tbuf[...] += tland[n]

    def down(s, some):
        reduce.down(s, some)
        if some is EARLY:
            table_land(s)
            if s < 3:
                table(s + 1).start()
        elif s == 3:
            for b in range(4, links.bits):
                table(b).start()
                table_land(b)
            for copy in touts:
                copy.start()
        if s == 3:
            for p in some:
                lanes = gather.lanes(p)
                gather.whole[gather.held(p, 4), lanes] = buf[gather.held(p, 4), lanes]
            gather.begin(some)

    touts = [
        pltpu.make_async_copy(tbuf, otab_hbm.at[near], tout.at[0]),
        remote(tbuf, otab_hbm.at[near], tout.at[1], tout.at[2], links.twin),
    ]

    for load in loads:
        load.wait()
    table(0).start()

    @pl.when(core == 0)
    def _():
        x[...] = MUON_KEEP * m1[...] + x[...]

    @pl.when(core == 1)
    def _():
        def flat(o):
            lanes = pl.ds(o, D)
            x[:, lanes] = MUON_KEEP * m2[lanes].T + x[:, lanes]

        sweep(wide, D, flat)

    inv = inverse_norm(x[...])
    chunks = [slice(o, o + 2 * PIECE) for o in range(0, wide, 2 * PIECE)]

    def keep(lanes, v):
        h, l = halves(v)
        xc[0:D, lanes] = h
        xc[D : 2 * D, lanes] = h
        xc[2 * D : 3 * D, lanes] = l

    def kept(lanes):
        return xc[0:D, lanes].astype(F32) + xc[2 * D : 3 * D, lanes].astype(F32)

    for lanes in chunks:
        keep(lanes, x[:, lanes] * inv)

    def gram():
        return gram_of(xc[0:D], xc[2 * D : 3 * D])

    schedule = {
        (0, 0): ((down, 0, LATE),),
        (0, 2): ((down, 1, EARLY),),
        (1, 0): ((down, 1, LATE),),
        (1, 1): ((down, 2, EARLY),),
        (1, 2): ((down, 2, LATE), (down, 3, EARLY)),
        (2, 0): ((down, 3, LATE),),
        (2, 1): ((gather.up, 3, EARLY),),
        (2, 2): ((gather.up, 3, LATE),),
        (3, 0): ((gather.up, 2, EARLY),),
        (3, 1): ((gather.up, 2, LATE),),
        (3, 2): ((gather.up, 1, EARLY),),
        (4, 0): ((gather.up, 1, LATE),),
    }

    def step(i, carry):
        def events(n):
            for turn in range(5):
                if (turn, n) in schedule:

                    @pl.when(i == turn)
                    def _():
                        for event, *args in schedule[turn, n]:
                            event(*args)

        g0 = gram()
        g = halves(g0)
        events(0)
        poly[...] = side(NS_B * g0 + NS_C * times_symmetric(g, g))
        events(1)

        def apply_to(o):
            lanes = pl.ds(pl.multiple_of(o, 2 * PIECE), 2 * PIECE)
            keep(lanes, NS_A * kept(lanes) + dot_nn(poly[...], xc[:, lanes]))

        sweep(wide, 2 * PIECE, apply_to)
        events(2)
        return carry

    down(0, EARLY)
    lax.fori_loop(0, 5, step, 0)
    for lanes in chunks:
        x[:, lanes] = kept(lanes)

    @pl.when(core == 0)
    def _():
        for b in range(blocks):
            xs[b] = x[:, b * D : b * D + D]

    @pl.when(core == 1)
    def _():
        def tall(o):
            xs[lax.div(o, D)] = x[:, pl.ds(o, D)].T

        sweep(wide, D, tall)

    orth = [
        pltpu.make_async_copy(xs, orth_hbm.at[core], tout.at[3]),
        remote(xs, orth_hbm.at[core], tout.at[4], tout.at[5], links.twin),
    ]
    for copy in orth:
        copy.start()
    gather.up(0, EARLY)
    gather.up(0, LATE)
    gather.end()
    for copy in touts + orth:
        copy.wait()


def wide_blocks(end, tab, mid, m1, m2):
    bits = (lax.axis_size("canvas") - 1).bit_length()
    anywhere = pl.BlockSpec(memory_space=pl.ANY)
    blocks = m1.shape[1] // D
    return pl.pallas_call(
        wide_kernel,
        out_shape=[
            jax.ShapeDtypeStruct((2,) + end.shape, F32),
            jax.ShapeDtypeStruct((TABLE, D), F32),
            jax.ShapeDtypeStruct((2, blocks, D, D), F32),
        ],
        in_specs=[anywhere] * 5,
        out_specs=[anywhere] * 3,
        scratch_shapes=[
            pltpu.VMEM((blocks, D, D), F32),
            pltpu.VMEM(m1.shape, F32),
            pltpu.VMEM(m1.shape, F32),
            pltpu.VMEM(m2.shape, F32),
            pltpu.VMEM((3 * D, m1.shape[1]), BF),
            pltpu.VMEM((D, 3 * D), BF),
            pltpu.VMEM((TABLE // 2, D), F32),
            pltpu.VMEM((bits, TABLE // 2, D), F32),
            DMA((4,)),
            DMA((bits,)),
            DMA((bits,)),
            DMA((6,)),
            pltpu.VMEM(end.shape, F32),
            DMA,
        ]
        + Reduce.scratch(end.shape[1], bits)
        + Gather.scratch(end.shape[1]),
        compiler_params=pltpu.CompilerParams(
            collective_id=2, has_side_effects=True, vmem_limit_bytes=60 << 20
        ),
    )(end, tab, mid, m1, m2)


def muon(w, orth, large):
    return w * (1.0 - MUON_RATE * DECAY) - MUON_RATE * 0.2 * math.sqrt(large) * orth


def square_kernel(
    end_hbm,
    mid_hbm,
    wide_hbm,
    mq_hbm,
    mp_hbm,
    m1_hbm,
    m2_hbm,
    w1_hbm,
    w2_hbm,
    out_hbm,
    dx_hbm,
    gq_out,
    gp_out,
    g1_out,
    g2_out,
    nq_out,
    np_out,
    n1_out,
    n2_out,
    w1_out,
    w2_out,
    c1_out,
    c2_out,
    out_out,
    dx_out,
    orth_hbm,
    end,
    mid,
    nat,
    mq,
    mp,
    m1,
    m2,
    w1,
    w2,
    c1,
    c2,
    wide,
    out,
    dx,
    xh,
    xl,
    xs,
    in_sem,
    out_sem,
):
    core = lax.axis_index("rows")
    mlp = m1.shape[1]
    blocks = mlp // D
    pairs = (
        (end_hbm, end),
        (mq_hbm, mq),
        (mp_hbm, mp),
        (mid_hbm, mid),
        (m1_hbm, m1),
        (m2_hbm, m2),
        (w1_hbm, w1),
        (w2_hbm, w2),
        (wide_hbm, wide),
        (out_hbm, out),
        (dx_hbm, dx),
    )
    loads = [pltpu.make_async_copy(a, b, in_sem.at[i]) for i, (a, b) in enumerate(pairs)]
    for load in loads:
        load.start()
    for load in loads[0:3]:
        load.wait()
    outs = (
        (end.at[0], gq_out.at[:, 0 : 2 * D]),
        (end.at[1, :, 0:D], gq_out.at[:, 2 * D : 3 * D]),
        (end.at[1, :, D : 2 * D], gp_out),
        (mq, nq_out),
        (mp, np_out),
        (mid.at[0], g1_out),
        (nat, g2_out),
        (m1, n1_out),
        (m2, n2_out),
        (out, out_out),
        (dx, dx_out),
        (w1, w1_out),
        (w2, w2_out),
        (c1, c1_out),
        (c2, c2_out),
        (xs, orth_hbm),
    )

    def store(*which):
        return [pltpu.make_async_copy(*outs[n], out_sem.at[n]) for n in which]

    def send(*which):
        for copy in store(*which):
            copy.start()

    send(0, 1, 2)

    def small(o):
        rows = pl.ds(o, 128)
        mq[rows, 0 : 2 * D] = MUON_KEEP * mq[rows, 0 : 2 * D] + end[0, rows]
        mq[rows, 2 * D : 3 * D] = MUON_KEEP * mq[rows, 2 * D : 3 * D] + end[1, rows, 0:D]
        mp[rows] = MUON_KEEP * mp[rows] + end[1, rows, D : 2 * D]

    sweep(D, 128, small)
    send(3, 4)

    def keep(b, v):
        xh[b], xl[b] = halves(v)

    @pl.when(core == 0)
    def _():
        xs[0] = mq[:, 0:D]
        xs[1] = mq[:, D : 2 * D]

    @pl.when(core == 1)
    def _():
        xs[0] = mq[:, 2 * D : 3 * D]
        xs[1] = mp[...]

    for b in range(2):
        keep(b, xs[b] * inverse_norm(xs[b]))

    def step(i, carry):
        x = [(xh[b], xl[b]) for b in range(2)]
        g = [gram_of(h, l) for h, l in x]
        pairs = [halves(v) for v in g]
        p = [NS_B * v + NS_C * times_symmetric(w, w) for v, w in zip(g, pairs)]
        pairs = [halves(v) for v in p]
        for b in range(2):
            h, l = x[b]
            keep(b, NS_A * (h.astype(F32) + l.astype(F32)) + times(pairs[b], x[b]))
        pl.when(i == 1)(moments)
        pl.when(i == 2)(weights)
        return carry

    def moments():
        for load in loads[3:6]:
            load.wait()
        send(5)

        def natural(o):
            nat[pl.ds(o, D)] = mid[1, :, pl.ds(o, D)].T

        sweep(mlp, D, natural)
        send(6)

        def large(o):
            rows = pl.ds(o, 64)
            m1[rows] = MUON_KEEP * m1[rows] + mid[0, rows]

        sweep(D, 64, large)
        send(7)

        def larger(o):
            rows = pl.ds(o, 256)
            m2[rows] = MUON_KEEP * m2[rows] + nat[rows]

        sweep(mlp, 256, larger)
        send(8)

    def weights():
        for load in loads[6:]:
            load.wait()
        send(9, 10)

        def block(o):
            at = pl.ds(o, D)
            b = lax.div(o, D)
            new = muon(w1[:, at], wide[0, b], mlp)
            w1[:, at] = new
            c1[:, at] = new.astype(BF)
            new = muon(w2[at], wide[1, b], mlp)
            w2[at] = new
            c2[at] = new.astype(BF)

        sweep(mlp, D, block)
        send(11, 12, 13, 14)

    lax.fori_loop(0, 5, step, 0)
    for b in range(2):
        xs[b] = xh[b].astype(F32) + xl[b].astype(F32)
    send(15)
    for copy in store(*range(len(outs))):
        copy.wait()


def square_blocks(end, mid, wide, mq, mp, m1, m2, w1, w2, out, dx):
    anywhere = pl.BlockSpec(memory_space=pl.ANY)

    def like(v, kind=F32):
        return jax.ShapeDtypeStruct(v.shape, kind)

    def room(v, kind=F32):
        return pltpu.VMEM(v.shape, kind)

    return pl.pallas_call(
        square_kernel,
        out_shape=[like(v) for v in (mq, mp, m1, m2, mq, mp, m1, m2, w1, w2)]
        + [like(w1, BF), like(w2, BF), like(out), like(dx), jax.ShapeDtypeStruct((2, D, D), F32)],
        in_specs=[anywhere] * 11,
        out_specs=[anywhere] * 15,
        scratch_shapes=[room(v) for v in (end, mid, m2, mq, mp, m1, m2, w1, w2)]
        + [room(w1, BF), room(w2, BF), room(wide), room(out), room(dx)]
        + [
            pltpu.VMEM((2, D, D), BF),
            pltpu.VMEM((2, D, D), BF),
            pltpu.VMEM((2, D, D), F32),
            DMA((11,)),
            DMA((16,)),
        ],
        compiler_params=pltpu.CompilerParams(vmem_limit_bytes=60 << 20),
    )(end, mid, wide, mq, mp, m1, m2, w1, w2, out, dx)


def trade_kernel(own_ref, peer_ref, send_sem, recv_sem):
    core = lax.axis_index("rows")
    twin = {"rows": 1 - core}
    barrier = pltpu.get_barrier_semaphore()
    pl.semaphore_signal(barrier, inc=1, device_id=twin, device_id_type=MESH_ID)
    pl.semaphore_wait(barrier, 1)
    copy = remote(own_ref, peer_ref, send_sem, recv_sem, twin)
    copy.start()
    copy.wait()


def trade(own):
    anywhere = pl.BlockSpec(memory_space=pl.ANY)
    return pl.pallas_call(
        trade_kernel,
        out_shape=jax.ShapeDtypeStruct(own.shape, F32),
        in_specs=[anywhere],
        out_specs=anywhere,
        scratch_shapes=[DMA, DMA],
        compiler_params=pltpu.CompilerParams(collective_id=3, has_side_effects=True),
    )(own)


def moment_step(current, one, two, gradient):
    first = BETA1 * one + (1.0 - BETA1) * gradient
    second = BETA2 * two + (1.0 - BETA2) * gradient * gradient
    fix_one = 1.0 - BETA1**STEP
    fix_two = 1.0 - BETA2**STEP
    updated = current - ADAM_RATE * (first / fix_one) / (jnp.sqrt(second / fix_two) + ADAM_FLOOR)
    return first, second, updated


def update_kernel(
    count,
    temp_ref,
    heat_one_ref,
    heat_two_ref,
    own_ref,
    peer_ref,
    wq_ref,
    wp_ref,
    tab_ref,
    one_ref,
    two_ref,
    gtab_ref,
    nq_ref,
    np_ref,
    cq_ref,
    cp_ref,
    first_ref,
    second_ref,
    small_ref,
    heat_first_ref,
    heat_second_ref,
    heat_ref,
    rms_ref,
):
    lower = lax.axis_index("rows") == 0
    own, peer = own_ref[...], peer_ref[...]
    low, high = jnp.where(lower, own, peer), jnp.where(lower, peer, own)
    for i, orth in enumerate((low[0], low[1], high[0])):
        lanes = slice(i * D, i * D + D)
        new = muon(wq_ref[:, lanes], orth, D)
        nq_ref[:, lanes] = new
        cq_ref[:, lanes] = new.astype(BF)
    new = muon(wp_ref[...], high[1], D)
    np_ref[...] = new
    cp_ref[...] = new.astype(BF)
    first, second, small = moment_step(tab_ref[...], one_ref[...], two_ref[...], gtab_ref[0:SMALL])
    first_ref[...] = first
    second_ref[...] = second
    small_ref[...] = small

    @pl.when(pl.program_id(0) == 0)
    def _():
        head = lax.broadcasted_iota(jnp.int32, (HEADS, D), 0)
        lane = lax.broadcasted_iota(jnp.int32, (HEADS, D), 1) // HD
        heat = jnp.sum(jnp.where(head == lane, gtab_ref[44:45], 0.0), axis=1, keepdims=True)
        head = lax.broadcasted_iota(jnp.int32, (HEADS, 1), 0)

        def column(ref):
            v = jnp.where(head == 0, ref[0], 0.0)
            for h in range(1, HEADS):
                v = jnp.where(head == h, ref[h], v)
            return v

        results = moment_step(column(temp_ref), column(heat_one_ref), column(heat_two_ref), heat)
        for ref, v in zip((heat_first_ref, heat_second_ref, heat_ref), results):
            for h in range(HEADS):
                ref[h] = v[h, 0]
        rms = jnp.sqrt(jnp.sum(gtab_ref[40:44], axis=1, keepdims=True) / count)
        for n in range(4):
            rms_ref[n] = rms[n, 0]


def update(count, temp, heat_one, heat_two, own, peer, wq, wp, tab, one, two, gtab):
    steps = 3
    piece = D // steps

    def rows(v):
        return pl.BlockSpec((piece, v.shape[1]), lambda i: (i, 0))

    def whole(v):
        return pl.BlockSpec(v.shape, lambda i: (0, 0))

    square = pl.BlockSpec((2, piece, D), lambda i: (0, i, 0))
    weights = (wq, wp)
    smem = pl.BlockSpec(memory_space=pltpu.SMEM)
    return pl.pallas_call(
        functools.partial(update_kernel, count),
        grid=(steps,),
        out_shape=[jax.ShapeDtypeStruct(w.shape, F32) for w in weights]
        + [jax.ShapeDtypeStruct(w.shape, BF) for w in weights]
        + [jax.ShapeDtypeStruct(tab.shape, F32)] * 3
        + [jax.ShapeDtypeStruct(temp.shape, F32)] * 3
        + [jax.ShapeDtypeStruct((4,), F32)],
        in_specs=[smem] * 3
        + [square, square]
        + [rows(w) for w in weights]
        + [whole(v) for v in (tab, one, two, gtab)],
        out_specs=[rows(w) for w in weights] * 2 + [whole(tab)] * 3 + [smem] * 4,
        compiler_params=pltpu.CompilerParams(vmem_limit_bytes=60 << 20),
    )(temp, heat_one, heat_two, own, peer, *weights, tab, one, two, gtab)


def on_device(
    x4, dy4, tall, wqkv, wp, w1, w2, mqkv, mp, m1, m2, tab, tab_one, tab_two, temp, temp_one, temp_two
):
    shape = x4.shape
    tokens = shape[1] * shape[2]
    x = x4.reshape(tokens, D)
    dy = dy4.reshape(tokens, D)
    q, k, v, sums = project(tall, x, wqkv, tab)
    out, ds1, dmx, dwp, shard, gtab, probs, unit, gprob, joint = middle(
        tall, temp, x, dy, v, sums, wp, w1, w2, tab
    )
    dx, end, gtab, mid = finish(
        tall, temp, x, q, k, ds1, dmx, sums, joint, probs, unit, gprob, wqkv, tab, gtab, dwp, shard
    )
    end, gtab, wide = wide_blocks(end, gtab, mid, m1, m2)
    *grads, new_1, new_2, copy_1, copy_2, out, dx, square = square_blocks(
        end, mid, wide, mqkv, mp, m1, m2, w1, w2, out, dx
    )
    count = tokens * D * lax.axis_size("rows") * lax.axis_size("canvas")
    new_q, new_p, copy_q, copy_p, *small = update(
        count, temp, temp_one, temp_two, square, trade(square), wqkv, wp, tab, tab_one, tab_two, gtab
    )
    new = (new_q, new_p, new_1, new_2, copy_q, copy_p, copy_1, copy_2)
    return (out.reshape(shape), dx.reshape(shape), *grads, *new, *small)


def solution(mesh):
    split = P("canvas", "rows", None, None)
    return jax.shard_map(
        on_device,
        mesh=mesh,
        in_specs=(split, split, P("canvas", None)) + (P(),) * 14,
        out_specs=(split, split) + (P(),) * 23,
        check_vma=False,
    )
```

profile of v0, /device:TPU:0, one launch (start us, length us, event | category | flops | bytes accessed | tf_op | source)
XLA Modules:
  0.0 211.1 jit_solution(2593937700871278302)
XLA Ops:
  0.7 12.0 %shard_map.360 = (f32[1024,384]{1,0:T(8,128)}, f32[1024,384]{1,0:T(8,128)}, f32[1024,384]{1,0:T(8,128)}, f32[3,56,384]{2,1,0:T(8,128)}) custom-call(s32[1,4]{1,0:T(1,128)} %tall_ref.5, f32[1024,384]{1,0:T(8,128)} %bitcast.4, f32[384,1152]{1,0:T(8,128)} %wq_ref.1, f32[40,384]{1,0:T(8,128)} %tab_ref.7), custom_call_target="tpu_custom_call" | custom-call | tf_op jit(solution)/shard_map/pallas_call | solution.py:244
  12.6 79.7 %shard_map.361 = (f32[1024,384]{1,0:T(8,128)}, f32[1024,384]{1,0:T(8,128)}, f32[1024,384]{1,0:T(8,128)}, f32[384,384]{1,0:T(8,128)}, f32[48,1536]{1,0:T(8,128)},...) custom-call(s32[1,4]{1,0:T(1,128)} %tall_ref.5, ...), custom_call_target="tpu_custom_call" | custom-call | tf_op jit(solution)/shard_map/pallas_call | solution.py:970
  92.3 42.0 %shard_map.362 = (f32[1024,384]{1,0:T(8,128)}, f32[384,768]{1,0:T(8,128)}, f32[24,384]{1,0:T(8,128)}, f32[2,384,1536]{2,1,0:T(8,128)}) custom-call(s32[1,4]{1,0:T(1,128)} %tall_ref.5, f32[8]{0:T(128)} %temp_ref.5, f32[1024,384]{1,0:T(8,128)} %bitcast.6, f32[1024,384]{1,0:T(8,128)} %get-tuple-element.72.q_ref, f32[1024,384]{1,0:T(8,128)} %get-tuple-element.73.k_ref, ...), custom_call_target="tpu_custom_call" | custom-call | tf_op jit(solution)/shard_map/pallas_call | solution.py:1204
  134.4 46.5 %shard_map.363 = (f32[2,384,768]{2,1,0:T(8,128)}, f32[48,384]{1,0:T(8,128)}, f32[2,4,384,384]{3,2,1,0:T(8,128)}) custom-call(f32[384,768]{1,0:T(8,128)} %get-tuple-element.85.end_hbm, f32[24,384]{1,0:T(8,128)} %get-tuple-element.86.tab_hbm, f32[2,384,1536]{2,1,0:T(8,128)} %get-tuple-element.87.mid_hbm, f32[384,1536]{1,0:T(8,128)} %m1_hbm.3, f32[1536,384]{1,0:T(8,128)} %m2_hbm.3), custom_call_target="tpu_custom_call" | custom-call | tf_op jit(solution)/shard_map/pallas_call | solution.py:1460
  180.9 21.3 %shard_map.364 = (f32[384,1152]{1,0:T(8,128)}, f32[384,384]{1,0:T(8,128)}, f32[384,1536]{1,0:T(8,128)}, f32[1536,384]{1,0:T(8,128)}, f32[384,1152]{1,0:T(8,128)}...) custom-call(f32[2,384,768]{2,1,0:T(8,128)} %get-tuple-element.88.end, ...), custom_call_target="tpu_custom_call" | custom-call | tf_op jit(solution)/shard_map/pallas_call | solution.py:1691
  202.2 3.2 %shard_map.365.peer_ref = f32[2,384,384]{2,1,0:T(8,128)} custom-call(f32[2,384,384]{2,1,0:T(8,128)} %get-tuple-element.102.own_ref), custom_call_target="tpu_custom_call" | custom-call | tf_op jit(solution)/shard_map/pallas_call | solution.py:1723
  205.4 5.4 %shard_map.366 = (f32[384,1152]{1,0:T(8,128)}, f32[384,384]{1,0:T(8,128)}, bf16[384,1152]{1,0:T(8,128)(2,1)}, bf16[384,384]{1,0:T(8,128)(2,1)}, f32[40,384]{1,0:...) custom-call(f32[8]{0:T(128)} %temp_ref.5, ...), custom_call_target="tpu_custom_call" | custom-call | tf_op jit(solution)/shard_map/pallas_call | solution.py:1818
where the time goes:
time: 211 us
  Pallas kernels  210 us (100%)
    pallas_call x1, Pallas kernels, middle(): pl.pallas_call(middle_kernel, out_shape=[f(tokens, D), f(tokens, D), f(to...  79.7 us
    pallas_call x1, Pallas kernels, wide_blocks(): pl.pallas_call(wide_kernel, out_shape=[jax.ShapeDtypeStruct((2,) + end.sh...  46.5 us
    pallas_call x1, Pallas kernels, finish(): pl.pallas_call(finish_kernel, grid=(tokens // TILE,), out_shape=[jax.Shap...  42 us
    pallas_call x1, Pallas kernels, square_blocks(): pl.pallas_call(square_kernel, out_shape=[like(v) for v in (mq, mp, m1, m2...  21.3 us
    pallas_call x1, Pallas kernels, project(): pl.pallas_call(project_kernel, grid=(tokens // TILE,), out_shape=[jax.Sha...  12 us
    pallas_call x1, Pallas kernels, update(): pl.pallas_call(functools.partial(update_kernel, count), grid=(steps,), ou...  5.41 us

commit v1 on v0

--- a/solution.py
+++ b/solution.py
@@ -660,10 +660,11 @@
     edges[0].wait()
     ones = group_ones()
     temp = head_row(temp_ref)
-    joint_ref[...] = sums_ref[2] + peer_ref[...]
-
-    def probabilities(s, carry):
-        sums = jnp.where(s == 2, joint_ref[...], sums_ref[s])
+    for s in range(3):
+        sums = sums_ref[s]
+        if s == 2:
+            sums = sums + peer_ref[...]
+            joint_ref[...] = sums
         inv_q = lax.rsqrt(sums[HD : HD + 1] + EPS)
         inv_k = lax.rsqrt(sums[HD + 1 : HD + 2] + EPS)
         unit = sums[0:HD] * row_to_fold(inv_q, ones) * inv_k
@@ -672,11 +673,7 @@
         probs = weight / group_sum(weight, ones)
         probs_ref[s] = probs
         h, l = halves(unfold(probs))
-        lanes = pl.ds(pl.multiple_of(3 * D * s, 128), 3 * D)
-        pcat[:, lanes] = jnp.concatenate([h, h, l], axis=1)
-        return carry
-
-    lax.fori_loop(0, 3, probabilities, 0)
+        pcat[:, 3 * s * D : 3 * s * D + 3 * D] = jnp.concatenate([h, h, l], axis=1)
 
     acc[...] = jnp.zeros_like(acc)
     gtab_ref[...] = jnp.zeros_like(gtab_ref)
@@ -910,15 +907,14 @@
         dwp_ref[...] += dot_nn(side(mixed[pl.ds(o, TILE)].T), jnp.concatenate([h, h, l], axis=0))
         cross[...] += dot_nn(side(dmx.T), slots_below(v_ref[pl.ds(o, TILE)], slot_masks(o, TILE, spans)))
 
-    def back_two(step, carry):
-        back(2 * step)
-        back(2 * step + 1)
+    def back_one(step, carry):
+        back(step)
         pl.when(step == 0)(lambda: reduce.down(0, LATE, 2))
-        pl.when(step == 0)(lambda: reduce.down(1, EARLY, 2))
+        pl.when(step == 1)(lambda: reduce.down(1, EARLY, 2))
+        pl.when(step == 2)(lambda: reduce.down(1, LATE, 2))
         return carry
 
-    lax.fori_loop(0, tokens // TILE // 2, back_two, 0)
-    reduce.down(1, LATE, 2)
+    lax.fori_loop(0, tokens // TILE, back_one, 0)
     for src, dst in ((slope, ds1_hbm), (act, dmx_hbm)):
         stores.append(pltpu.make_async_copy(src.at[own], dst, store_sem.at[len(stores)]))
         stores[-1].start()
@@ -1094,34 +1090,31 @@
         acc[...] = jnp.zeros_like(acc)
         ones = group_ones()
         temp = head_row(temp_ref)
-        swap.wait()
-
-        def slot(s, heat):
-            sums = jnp.where(s == 2, peer_ref[...], sums_ref[s])
-            grad = gprob_ref[s] + jnp.where(s == 2, gpeer_ref[...], 0.0)
+        heat = jnp.zeros((1, D), F32)
+        for s in range(3):
+            sums = sums_ref[s]
+            grad = gprob_ref[s]
+            if s == 2:
+                swap.wait()
+                sums = peer_ref[...]
+                grad = grad + gpeer_ref[...]
             inv_q = lax.rsqrt(sums[HD : HD + 1] + EPS)
             inv_k = lax.rsqrt(sums[HD + 1 : HD + 2] + EPS)
             probs = probs_ref[s]
             unit = unit_ref[s]
             scores = probs * (grad - group_sum(probs * grad, ones))
             part_heat = jnp.sum(scores * unit, axis=0, keepdims=True)
-            heat = heat + jnp.where((s < 2) | (core == 0), part_heat, 0.0)
+            heat = heat + (part_heat if s < 2 else jnp.where(core == 0, part_heat, 0.0))
             pull = temp * scores
             both = pull * unit
-            query = fold_to_row(group_sum(both, ones)) * inv_q * inv_q
-            key = jnp.sum(both, axis=0, keepdims=True) * inv_k * inv_k
-            side_rows[pl.ds(pl.multiple_of(8 * s, 8), 8)] = jnp.concatenate(
-                [query, key, jnp.zeros((6, D), F32)], axis=0
-            )
-            across = pl.ds(pl.multiple_of(3 * D * s, 128), 3 * D)
+            side_rows[8 * s : 8 * s + 1] = fold_to_row(group_sum(both, ones)) * inv_q * inv_q
+            side_rows[8 * s + 1 : 8 * s + 2] = jnp.sum(both, axis=0, keepdims=True) * inv_k * inv_k
+            across = slice(3 * s * D, 3 * s * D + 3 * D)
             h, l = halves(unfold(pull * row_to_fold(inv_q, ones) * inv_k))
             cv[across] = jnp.concatenate([h, h, l], axis=0)
             ch[:, across] = jnp.concatenate([h, h, l], axis=1)
             h, l = halves(unfold(probs))
             pv[across] = jnp.concatenate([h, h, l], axis=0)
-            return heat
-
-        heat = lax.fori_loop(0, 3, slot, jnp.zeros((1, D), F32))
         otab_ref[...] = gtab_ref[...]
         otab_ref[44:45] = heat
 

time: 211 us -> 208 us (0.986)
  Pallas kernels: 210 us -> 206 us
    pallas_call x1, Pallas kernels: 42 us -> 39.8 us  [finish(): pl.pallas_call(finish_kernel, grid=(tokens // TILE,), out_shape=[jax.Shap...]
where the time goes in v1:
time: 208 us; the launch traced here: 207 us
  Pallas kernels  206 us (99%)
    pallas_call x1, Pallas kernels, middle(): pl.pallas_call(middle_kernel, out_shape=[f(tokens, D), f(tokens, D), f(to...  78.7 us
    pallas_call x1, Pallas kernels, wide_blocks(): pl.pallas_call(wide_kernel, out_shape=[jax.ShapeDtypeStruct((2,) + end.sh...  46.3 us
    pallas_call x1, Pallas kernels, finish(): pl.pallas_call(finish_kernel, grid=(tokens // TILE,), out_shape=[jax.Shap...  39.8 us
    pallas_call x1, Pallas kernels, square_blocks(): pl.pallas_call(square_kernel, out_shape=[like(v) for v in (mq, mp, m1, m2...  21.1 us
    pallas_call x1, Pallas kernels, project(): pl.pallas_call(project_kernel, grid=(tokens // TILE,), out_shape=[jax.Sha...  12 us
    pallas_call x1, Pallas kernels, update(): pl.pallas_call(functools.partial(update_kernel, count), grid=(steps,), ou...  5.41 us

profile of v1, /device:TPU:0, one launch (start us, length us, event | category | flops | bytes accessed | tf_op | source)
XLA Modules:
  0.0 207.4 jit_solution(6054171046669535702)
XLA Ops:
  0.7 12.0 %shard_map.360 = (f32[1024,384]{1,0:T(8,128)}, f32[1024,384]{1,0:T(8,128)}, f32[1024,384]{1,0:T(8,128)}, f32[3,56,384]{2,1,0:T(8,128)}) custom-call(s32[1,4]{1,0:T(1,128)} %tall_ref.5, f32[1024,384]{1,0:T(8,128)} %bitcast.4, f32[384,1152]{1,0:T(8,128)} %wq_ref.1, f32[40,384]{1,0:T(8,128)} %tab_ref.7), custom_call_target="tpu_custom_call" | custom-call | tf_op jit(solution)/shard_map/pallas_call | solution.py:244
  12.6 78.7 %shard_map.361 = (f32[1024,384]{1,0:T(8,128)}, f32[1024,384]{1,0:T(8,128)}, f32[1024,384]{1,0:T(8,128)}, f32[384,384]{1,0:T(8,128)}, f32[48,1536]{1,0:T(8,128)},...) custom-call(s32[1,4]{1,0:T(1,128)} %tall_ref.5, ...), custom_call_target="tpu_custom_call" | custom-call | tf_op jit(solution)/shard_map/pallas_call | solution.py:966
  91.4 39.8 %shard_map.362 = (f32[1024,384]{1,0:T(8,128)}, f32[384,768]{1,0:T(8,128)}, f32[24,384]{1,0:T(8,128)}, f32[2,384,1536]{2,1,0:T(8,128)}) custom-call(s32[1,4]{1,0:T(1,128)} %tall_ref.5, f32[8]{0:T(128)} %temp_ref.5, f32[1024,384]{1,0:T(8,128)} %bitcast.6, f32[1024,384]{1,0:T(8,128)} %get-tuple-element.72.q_ref, f32[1024,384]{1,0:T(8,128)} %get-tuple-element.73.k_ref, ...), custom_call_target="tpu_custom_call" | custom-call | tf_op jit(solution)/shard_map/pallas_call | solution.py:1197
  131.2 46.3 %shard_map.363 = (f32[2,384,768]{2,1,0:T(8,128)}, f32[48,384]{1,0:T(8,128)}, f32[2,4,384,384]{3,2,1,0:T(8,128)}) custom-call(f32[384,768]{1,0:T(8,128)} %get-tuple-element.85.end_hbm, f32[24,384]{1,0:T(8,128)} %get-tuple-element.86.tab_hbm, f32[2,384,1536]{2,1,0:T(8,128)} %get-tuple-element.87.mid_hbm, f32[384,1536]{1,0:T(8,128)} %m1_hbm.3, f32[1536,384]{1,0:T(8,128)} %m2_hbm.3), custom_call_target="tpu_custom_call" | custom-call | tf_op jit(solution)/shard_map/pallas_call | solution.py:1453
  177.5 21.1 %shard_map.364 = (f32[384,1152]{1,0:T(8,128)}, f32[384,384]{1,0:T(8,128)}, f32[384,1536]{1,0:T(8,128)}, f32[1536,384]{1,0:T(8,128)}, f32[384,1152]{1,0:T(8,128)}...) custom-call(f32[2,384,768]{2,1,0:T(8,128)} %get-tuple-element.88.end, ...), custom_call_target="tpu_custom_call" | custom-call | tf_op jit(solution)/shard_map/pallas_call | solution.py:1684
  198.5 3.2 %shard_map.365.peer_ref = f32[2,384,384]{2,1,0:T(8,128)} custom-call(f32[2,384,384]{2,1,0:T(8,128)} %get-tuple-element.102.own_ref), custom_call_target="tpu_custom_call" | custom-call | tf_op jit(solution)/shard_map/pallas_call | solution.py:1716
  201.8 5.4 %shard_map.366 = (f32[384,1152]{1,0:T(8,128)}, f32[384,384]{1,0:T(8,128)}, bf16[384,1152]{1,0:T(8,128)(2,1)}, bf16[384,384]{1,0:T(8,128)(2,1)}, f32[40,384]{1,0:...) custom-call(f32[8]{0:T(128)} %temp_ref.5, ...), custom_call_target="tpu_custom_call" | custom-call | tf_op jit(solution)/shard_map/pallas_call | solution.py:1811
